TPU v7x, 1024 devices: a whole 8x8x8 slice. The times are simulated.
1024 devices in a mesh: space: 8 (over y), modej: 8 (over z), modek: 16 (over x, core).
Axes of the slice: x: 8, y: 8, z: 8, core: 2. Of those that a mesh axis runs over, the one named last changes fastest.
Arguments:
- mode_shapes: bfloat16 [3, 1024, 512], P(None, 'space', ('modej', 'modek')), may hold values from -6 to 6
- mode_grads: bfloat16 [8, 1024, 512], P(None, 'space', 'modek'), may hold values from -6 to 6
- cell_weights: float32 [1024], P('space'), may hold values from 0.005 to 0.03
Outputs:
- galerkin: bfloat16 [512, 512, 512], P('modek', ('space', 'modej'))
All inputs are finite; a program needn't handle non-finite values.
Results may differ from a plain program's by a relative error of at most 0.017.
Values may be sent and summed in bfloat16 or wider, within the bound.
A program may use at most 64 MiB of HBM per device.

v0:
```python
import jax
import jax.numpy as jnp
from jax import lax
from jax.sharding import PartitionSpec as P


def full_gradient(grad_piece):
    values = grad_piece.astype(jnp.float32)
    last = -(values[0] + values[4])
    return jnp.concatenate([values, last[None]], axis=0)


def convect_terms(shape_cols, grad_piece, weights):
    gradient = full_gradient(grad_piece)
    columns = shape_cols.astype(jnp.float32)
    rows_list = []
    for comp in range(3):
        total = columns[0][:, :, None] * gradient[comp * 3][:, None, :]
        total = total + columns[1][:, :, None] * gradient[comp * 3 + 1][:, None, :]
        total = total + columns[2][:, :, None] * gradient[comp * 3 + 2][:, None, :]
        rows_list.append(total * weights[:, None, None])
    return jnp.stack(rows_list, axis=0).astype(jnp.bfloat16)


def tensor_tile(shape_rows, shape_cols, grad_piece, weights):
    cells = shape_rows.shape[1]
    convect = convect_terms(shape_cols, grad_piece, weights)
    right = convect.reshape(3 * cells, shape_cols.shape[2] * grad_piece.shape[2])
    left = shape_rows.reshape(3 * cells, shape_rows.shape[2])
    product = lax.dot_general(
        left, right, (((0,), (0,)), ((), ())), preferred_element_type=jnp.float32
    )
    return product.reshape(shape_rows.shape[2], shape_cols.shape[2], grad_piece.shape[2]).astype(
        jnp.bfloat16
    )


def body(mode_shapes, mode_grads, cell_weights):
    all_shapes = lax.all_gather(mode_shapes, ("modej", "modek"), axis=2, tiled=True)
    total_modes = all_shapes.shape[2]
    cells = all_shapes.shape[1]
    space_count = lax.axis_size("space")
    second_groups = lax.axis_size("modej")
    owner_width = total_modes // (space_count * second_groups)
    grouped = all_shapes.reshape(3, cells, space_count, second_groups, owner_width)
    picked = lax.dynamic_slice_in_dim(grouped, lax.axis_index("modej"), 1, 3)
    second_shapes = picked.reshape(3, cells, space_count * owner_width)
    block_tiles = tensor_tile(all_shapes, second_shapes, mode_grads, cell_weights)
    tiles = lax.all_to_all(block_tiles, "modek", split_axis=0, concat_axis=2, tiled=True)
    summed = lax.psum_scatter(
        tiles.astype(jnp.float32).astype(jnp.bfloat16), "space", scatter_dimension=1, tiled=True
    )
    return summed


def solution(mesh):
    in_specs = (P(None, "space", ("modej", "modek")), P(None, "space", "modek"), P("space"))
    out_specs = P("modek", ("space", "modej"), None)
    return jax.shard_map(body, mesh=mesh, in_specs=in_specs, out_specs=out_specs, check_vma=False)
```

profile of v0, /device:TPU:1, one launch (start us, length us, event | category | flops | bytes accessed | tf_op | source)
XLA Modules:
  0.0 218.1 jit_solution(15273271169637768126)
XLA Ops:
  6.5 0.0 copy-start
  6.5 0.0 reduce-scatter.2.cloned.1.call-start
  6.5 0.9 convert_element_type.30
  7.4 0.7 copy.28
  8.1 64.8 %all_gather.3 = bf16[3,128,512]{1,0,2:T(4,128)(2,1)S(1)} all-gather(bf16[3,128,4]{1,0,2:T(4,128)(2,1)S(1)} %copy.28), channel_id=1, replica_groups=mesh['space'=8,'modej'=8,'modek'=16] {'modej','modek'}, dimensions={2}, use_global_device_ids=true | all-gather | bytes 396288 | tf_op jit(solution)/shard_map/all_gather | solution.py:39
  72.9 0.3 copy.30
  73.2 0.1 copy.29
  73.3 0.0 copy-done
  73.3 5.8 %multiply_convert_fusion.2 = (bf16[1,128,64,32]{1,0,3,2:T(2,128)(2,1)S(1)}, bf16[1,128,64,32]{1,0,3,2:T(2,128)(2,1)S(1)}, bf16[1,128,64,32]{1,0,3,2:T(2,128)(2,1)S(1)}) fusion(f32[128]{0:T(128)S(1)} %copy-done, f32[128,32]{0,1:T(8,128)S(1)} %get-tuple-element.11, f32[128,64]{0,1:T(8,128)S(1)} %get-tuple-element.17, f32[128,32]{0,1:T(8,128)S(1)} %get-tuple-element.12, ...), kind=kLoop, calls=%fused_computation.6 | loop fusion | flops 5505024 | bytes 1819136 | tf_op jit(solution)/shard_map/convert
  79.1 3.6 %pad_maximum_fusion = bf16[3,128,64,32]{1,0,3,2:T(4,128)(2,1)S(1)} fusion(bf16[1,128,64,32]{1,0,3,2:T(2,128)(2,1)S(1)} %get-tuple-element.15, bf16[1,128,64,32]{1,0,3,2:T(2,128)(2,1)S(1)} %get-tuple-element.14, bf16[1,128,64,32]{1,0,3,2:T(2,128)(2,1)S(1)} %get-tuple-element.13), kind=kLoop, calls=%fused_computation.1 | loop fusion | flops 4718592 | bytes 3145728 | tf_op jit(solution)/shard_map/stack | solution.py:22
  82.7 1.3 convolution_convert_fusion
  84.0 7.8 %copy.31 = bf16[512,64,32]{1,2,0:T(8,128)(2,1)} copy(bf16[512,64,32]{0,2,1:T(8,128)(2,1)S(1)} %bitcast.48) | data formatting | bytes 4194304 | tf_op jit(solution)/shard_map/convert_element_type | solution.py:33
  91.8 6.3 %reshape.103 = bf16[16,2,32768]{2,1,0:T(2,128)(2,1)S(1)} reshape(bf16[512,32,64]{2,1,0:T(8,128)(2,1)} %bitcast.45) | data formatting | bytes 4194304
  98.1 56.8 %all_to_all.18 = bf16[16,2,32768]{2,1,0:T(2,128)(2,1)} all-to-all(bf16[16,2,32768]{2,1,0:T(2,128)(2,1)S(1)} %reshape.103), channel_id=1, replica_groups=mesh['space'=8,'modej'=8,'modek'=16] {'modek'}, dimensions={0} | all-to-all | bytes 4194304 | tf_op jit(solution)/shard_map/all_to_all | solution.py:49
  154.9 7.4 %reshape.104 = bf16[512,32,64]{2,1,0:T(8,128)(2,1)} reshape(bf16[16,2,32768]{2,1,0:T(2,128)(2,1)} %all_to_all.18) | data formatting | bytes 4194304
  162.3 5.4 %copy.32 = bf16[32,64,16,32]{1,3,2,0:T(8,128)(2,1)} copy(bf16[32,64,16,32]{1,3,0,2:T(8,128)(2,1)} %bitcast.46) | data formatting | bytes 4194304 | tf_op jit(solution)/shard_map/all_to_all | solution.py:49
  167.7 5.7 %copy.33 = bf16[32,64,512]{2,0,1:T(8,128)(2,1)} copy(bf16[32,64,512]{1,2,0:T(8,128)(2,1)} %bitcast.47) | data formatting | bytes 4194304 | tf_op jit(solution)/shard_map/all_to_all | solution.py:49
  173.4 0.0 reduce-scatter.2.cloned.1.call-update
  173.4 36.1 %reduce-scatter.2.cloned.1.call-done = bf16[32,8,512]{2,0,1:T(8,128)(2,1)} async-done(((bf16[32,64,512]{2,0,1:T(8,128)(2,1)}), bf16[32,8,512]{2,0,1:T(8,128)(2,1)}) %reduce-scatter.2.cloned.1.call-update) | async-done | bytes 262160 | tf_op jit(solution)/shard_map/reduce_scatter | solution.py:50
  209.5 1.8 copy.34
  (4 shorter events, 0.0 us)
Async XLA Ops:
  6.5 66.8 %copy-start = (f32[128]{0:T(128)S(1)}, f32[128]{0:T(128)}, u32[]{:S(2)}) copy-start(f32[128]{0:T(128)} %param.5) | copy-start | bytes 1540
  6.5 202.9 %reduce-scatter.2.cloned.1.call-start = ((), (), s32[]{:S(2)}) async-start(), calls=%async_computation.2 | async-start | bytes 2359296 | tf_op jit(solution)/shard_map/reduce_scatter | solution.py:50
Sparse Core Ops, SparseCore 0:
  173.5 35.9 reduce-scatter.1
where the time goes:
time: 222 us; the launch traced here: 218 us
  blocking collectives  122 us (55%)
  waiting for transfers between devices  36.1 us (16%)
  local copies, waits for them, and re-layouts  35.5 us (16%)
  between operations  13.5 us (6%)
  other arithmetic  10.2 us (5%)
    all_gather x1, blocking collectives, body(): lax.all_gather(mode_shapes, ('modej', 'modek'), axis=2, tiled=True)  64.8 us
    all_to_all x1, blocking collectives, body(): lax.all_to_all(block_tiles, 'modek', split_axis=0, concat_axis=2, tiled=T...  56.8 us
    reduce_scatter x1, waiting for transfers between devices, body(): lax.psum_scatter(tiles.astype(jnp.float32).astype(jnp.bfloat16), 'space',...  36.1 us
    unnamed x5, local copies, waits for them, and re-layouts  14.4 us
    all_to_all x2, local copies, waits for them, and re-layouts, body(): lax.all_to_all(block_tiles, 'modek', split_axis=0, concat_axis=2, tiled=T...  11.1 us
    convert_element_type x1, local copies, waits for them, and re-layouts, tensor_tile(): product.reshape(shape_rows.shape[2], shape_cols.shape[2], grad_piece.shap...  7.83 us
    another operation x1, other arithmetic  5.77 us
  transfers between devices with their start and end apart: 1, of which 1 were waited for; matrix products, arithmetic and copies ran while one was open for 0% of the time, Pallas kernels for 0%

commit v1 on v0

v1 whole, which is shorter than its diff:
```python
import functools

import jax
import jax.numpy as jnp
from jax import lax
from jax.experimental import pallas as pl
from jax.experimental.pallas import tpu as pltpu
from jax.sharding import PartitionSpec as P

MESH = pl.DeviceIdType.MESH
BF = jnp.bfloat16
F32 = jnp.float32
LANES = 128
NT = (((1,), (1,)), ((), ()))


def kernel(
    n,
    phi_ref,
    grad_ref,
    weight_ref,
    out_ref,
    own_phi,
    grads,
    second,
    first,
    left,
    right,
    sent,
    landed,
    tidy,
    send,
    recv_i1,
    recv_j1,
    recv_i2,
    recv_j2,
    recv_im,
    recv_jm,
    recv_g,
    recv_o,
    ready,
):
    y = lax.axis_index("space")
    z = lax.axis_index("modej")
    mk = lax.axis_index("modek")
    x = mk // 2
    c = mk % 2
    half = n // 2

    def at(yy, zz, xx, cc):
        return (yy, zz, xx * 2 + cc)

    def step(v, d):
        return lax.rem(v + d, n)

    def remote(src, dst, ssem, rsem, dev):
        return pltpu.make_async_remote_copy(
            src_ref=src, dst_ref=dst, send_sem=ssem, recv_sem=rsem, device_id=dev, device_id_type=MESH
        )

    def took(ref, sem):
        pltpu.make_async_copy(ref, ref, sem).wait()

    barrier = pltpu.get_barrier_semaphore()

    def hello(dev):
        pl.semaphore_signal(barrier, inc=1, device_id=dev, device_id_type=MESH)

    for d in range(1, n):
        hello(at(step(y, d), z, x, c))
        hello(at(step(y, d), z, x, 1 - c))
        hello(at(y, z, step(x, d), c))
        hello(at(y, step(z, d), x, c))
    hello(at(y, z, x, 1 - c))
    for t in range(n):
        @pl.when(jnp.logical_not((x == z) & (y == t)))
        def _():
            hello(at(t, x, z, c))

        @pl.when(jnp.logical_not((x == y) & (y == t)))
        def _():
            hello(at(t, z, y, c))

    rows = [jnp.transpose(phi_ref[a].astype(F32), (1, 0)) for a in range(3)]
    rows.append(jnp.zeros((4, LANES), F32))
    own_phi[...] = jnp.concatenate(rows, axis=0).astype(BF)
    weight = weight_ref[...]
    for ab in range(8):
        piece = jnp.transpose(grad_ref[ab].astype(F32), (1, 0)) * weight
        grads[y, ab * 32 : ab * 32 + 32, :] = piece.astype(BF)

    same_xz = (x == z).astype(jnp.int32)
    same_xy = (x == y).astype(jnp.int32)
    pl.semaphore_wait(barrier, 4 * (n - 1) + 1 + 2 * n - same_xz - same_xy)

    for d in range(1, n):
        pl.semaphore_signal(ready, inc=1, device_id=at(y, z, step(x, d), c), device_id_type=MESH)

    for t in range(n):
        self_i = (x == y) & (x == t)

        @pl.when(self_i)
        def _():
            pltpu.make_async_copy(own_phi, first.at[c, z, y], recv_i1).start()

        @pl.when(jnp.logical_not(self_i))
        def _():
            remote(own_phi, first.at[c, z, y], send.at[0], recv_i1, at(x, z, t, c)).start()

        self_j = (x == z) & (y == t)

        @pl.when(self_j)
        def _():
            pltpu.make_async_copy(own_phi, second.at[c, z, y], recv_j1).start()

        @pl.when(jnp.logical_not(self_j))
        def _():
            remote(own_phi, second.at[c, z, y], send.at[1], recv_j1, at(t, x, z, c)).start()

    for d in range(1, n):
        remote(grads.at[y], grads.at[y], send.at[6], recv_g.at[y], at(step(y, d), z, x, c)).start()

    took(first.at[c, z], recv_i1)
    for d in range(1, n):
        remote(first.at[c, z], first.at[c, z], send.at[2], recv_i2.at[z], at(y, step(z, d), x, c)).start()
    remote(first.at[c, z], first.at[c, z], send.at[4], recv_im.at[z], at(y, z, x, 1 - c)).start()
    took(second.at[c, x], recv_j1)
    for d in range(1, n):
        remote(second.at[c, x], second.at[c, x], send.at[3], recv_j2.at[x], at(y, z, step(x, d), c)).start()
    remote(second.at[c, x], second.at[c, x], send.at[5], recv_jm.at[x], at(y, z, x, 1 - c)).start()

    def turn(t):
        return lax.rem(jnp.where(t % 2 == 1, (t + 1) // 2, n - t // 2), n)

    def pass_i(t, carry):
        zs = step(z, turn(t))
        took(first.at[c, zs], recv_i2.at[zs])
        remote(first.at[c, zs], first.at[c, zs], send.at[4], recv_im.at[zs], at(y, z, x, 1 - c)).start()
        return carry

    lax.fori_loop(1, n, pass_i, 0)

    row_of = lax.broadcasted_iota(jnp.int32, (16, LANES), 0) // 4
    picks = [jnp.where(row_of == a, 1.0, 0.0).astype(BF) for a in range(3)]

    def build(t, carry):
        zs = step(z, turn(t))
        took(first.at[1 - c, zs], recv_im.at[zs])
        for cs in range(2):
            for ys in range(n):
                block = first[cs, zs, ys]
                for a in range(3):
                    at_row = pl.multiple_of(zs * 32 + cs * 16, 16)
                    left[pl.ds(at_row, 16), (ys * 3 + a) * LANES : (ys * 3 + a + 1) * LANES] = block * picks[a]
        return carry

    lax.fori_loop(0, n, build, 0)

    def await_g(d, carry):
        ys = step(y, d)
        took(grads.at[ys], recv_g.at[ys])
        return carry

    lax.fori_loop(1, n, await_g, 0)
    pl.semaphore_wait(ready, n - 1)
    owner_core = y // half
    place = lax.rem(y, half)
    low = lax.broadcasted_iota(jnp.int32, (8, 256), 0) < 4

    def chunk(t, carry):
        zs = step(x, turn(t))

        @pl.when(t < n - 1)
        def _():
            zn = step(x, turn(t + 1))
            took(second.at[c, zn], recv_j2.at[zn])
            remote(second.at[c, zn], second.at[c, zn], send.at[5], recv_jm.at[zn], at(y, z, x, 1 - c)).start()

        took(second.at[1 - c, zs], recv_jm.at[zs])

        for ys in range(n):
            g = [grads[ys, ab * 32 : ab * 32 + 32, :] for ab in range(8)]
            g.append(-(g[0] + g[4]))
            for cs in range(2):
                values = second[cs, zs, ys].astype(F32)
                for r in range(4):
                    v = [
                        jnp.broadcast_to(values[b * 4 + r : b * 4 + r + 1], (32, LANES)).astype(BF)
                        for b in range(3)
                    ]
                    for a in range(3):
                        total = v[0] * g[3 * a] + v[1] * g[3 * a + 1] + v[2] * g[3 * a + 2]
                        right[
                            (cs * 4 + r) * 32 : (cs * 4 + r) * 32 + 32,
                            (ys * 3 + a) * LANES : (ys * 3 + a + 1) * LANES,
                        ] = total
        product = lax.dot_general(left[...], right[...], NT, preferred_element_type=F32)
        for xd in range(n):
            parts = []
            for cs in range(2):
                base = xd * 32 + cs * 16
                both = product[base : base + 8] + product[base + 8 : base + 16]
                parts.append(both + pltpu.roll(both, 4, 0))
            tile = jnp.where(low, parts[0], parts[1])
            tile = jnp.concatenate([tile[:, :LANES], tile[:, LANES:]], axis=0)
            slot = zs * n + xd
            sent[slot] = tile.astype(BF)
            mine = (zs == y) & (x == xd) & (owner_core == c)

            @pl.when(mine)
            def _():
                pltpu.make_async_copy(sent.at[slot], landed.at[x, place, c], recv_o).start()

            @pl.when(jnp.logical_not(mine))
            def _():
                remote(
                    sent.at[slot], landed.at[x, place, c], send.at[7], recv_o, at(zs, z, xd, owner_core)
                ).start()
        return carry

    lax.fori_loop(0, n, chunk, 0)

    @pl.when(same_xy == 1)
    def _():
        took(first.at[0, 0, pl.ds(0, n - 1)], send.at[0])

    @pl.when(same_xy == 0)
    def _():
        took(first.at[0, 0], send.at[0])

    @pl.when(same_xz == 1)
    def _():
        took(second.at[0, 0, pl.ds(0, n - 1)], send.at[1])

    @pl.when(same_xz == 0)
    def _():
        took(second.at[0, 0], send.at[1])

    took(first.at[0, pl.ds(0, n - 1)], send.at[2])
    took(second.at[0, pl.ds(0, n - 1)], send.at[3])
    took(first.at[0], send.at[4])
    took(second.at[0], send.at[5])
    took(grads.at[pl.ds(0, n - 1)], send.at[6])

    @pl.when(owner_core == c)
    def _():
        took(sent.at[pl.ds(0, n * n - 1)], send.at[7])

    @pl.when(owner_core != c)
    def _():
        took(sent, send.at[7])

    took(landed, recv_o)

    lane = lax.broadcasted_iota(jnp.int32, (8, LANES), 1) // 32
    for p in range(half):
        for q in range(half):
            got = [landed[2 * q + s // 2, p, s % 2].astype(F32) for s in range(4)]
            for h in range(2):
                pieces = [g[h * 8 : h * 8 + 8] for g in got]
                for jl in range(4):
                    tile = pieces[jl]
                    for s in range(4):
                        if s != jl:
                            tile = jnp.where(lane == s, pltpu.roll(pieces[s], ((s - jl) * 32) % LANES, 1), tile)
                    tidy[q, pl.ds(p * 64 + h * 4 + jl, 8, stride=8), :] = tile
    for i in range(4 * n):
        for q in range(half):
            out_ref[i, :, q * LANES : (q + 1) * LANES] = tidy[q, i * 8 : i * 8 + 8, :].astype(BF)


def body(n, mode_shapes, mode_grads, cell_weights):
    vmem = pl.BlockSpec(memory_space=pltpu.VMEM)
    dma = pltpu.SemaphoreType.DMA
    return pl.pallas_call(
        functools.partial(kernel, n),
        out_shape=jax.ShapeDtypeStruct((4 * n, 8, 64 * n), BF),
        in_specs=[vmem] * 3,
        out_specs=vmem,
        scratch_shapes=[
            pltpu.VMEM((16, LANES), BF),
            pltpu.VMEM((n, 256, LANES), BF),
            pltpu.VMEM((2, n, n, 16, LANES), BF),
            pltpu.VMEM((2, n, n, 16, LANES), BF),
            pltpu.VMEM((32 * n, 3 * n * LANES), BF),
            pltpu.VMEM((256, 3 * n * LANES), BF),
            pltpu.VMEM((n * n, 16, LANES), BF),
            pltpu.VMEM((n, n // 2, 2, 16, LANES), BF),
            pltpu.VMEM((n // 2, 32 * n, LANES), F32),
            dma((8,)),
            dma(()),
            dma(()),
            dma((n,)),
            dma((n,)),
            dma((n,)),
            dma((n,)),
            dma((n,)),
            dma(()),
            pltpu.SemaphoreType.REGULAR,
        ],
        compiler_params=pltpu.CompilerParams(
            collective_id=0, has_side_effects=True, vmem_limit_bytes=40 * 2**20
        ),
    )(mode_shapes, mode_grads, cell_weights.reshape(1, -1))


def solution(mesh):
    n = mesh.shape["space"]
    in_specs = (P(None, "space", ("modej", "modek")), P(None, "space", "modek"), P("space"))
    out_specs = P("modek", ("space", "modej"), None)
    return jax.shard_map(
        functools.partial(body, n), mesh=mesh, in_specs=in_specs, out_specs=out_specs, check_vma=False
    )
```

time: 222 us -> 58.7 us (0.26); the launches traced: 218 us -> 58.5 us
  blocking collectives: 122 us -> 0 us
  Pallas kernels: 0 us -> 56.2 us
  waiting for transfers between devices: 36.1 us -> 0 us
  local copies, waits for them, and re-layouts: 35.5 us -> 2.24 us
  between operations: 13.5 us -> 0.03 us
  other arithmetic: 10.2 us -> 0 us
    all_gather x1 -> x0, blocking collectives: 64.8 us -> none  [body(): lax.all_gather(mode_shapes, ('modej', 'modek'), axis=2, tiled=True)]
    all_to_all x1 -> x0, blocking collectives: 56.8 us -> none  [body(): lax.all_to_all(block_tiles, 'modek', split_axis=0, concat_axis=2, tiled=T...]
    pallas_call x0 -> x1, Pallas kernels: none -> 56.2 us  [body(): pl.pallas_call(functools.partial(kernel, n), out_shape=jax.ShapeDtypeStru...]
    reduce_scatter x1 -> x0, waiting for transfers between devices: 36.1 us -> none  [body(): lax.psum_scatter(tiles.astype(jnp.float32).astype(jnp.bfloat16), 'space',...]
    unnamed x5 -> x7, local copies, waits for them, and re-layouts: 14.4 us -> 2.24 us
    all_to_all x2 -> x0, local copies, waits for them, and re-layouts: 11.1 us -> none  [body(): lax.all_to_all(block_tiles, 'modek', split_axis=0, concat_axis=2, tiled=T...]
    another operation x2 -> x0, other arithmetic: 9.34 us -> none
    convert_element_type x1 -> x0, local copies, waits for them, and re-layouts: 7.83 us -> none  [tensor_tile(): product.reshape(shape_rows.shape[2], shape_cols.shape[2], grad_piece.shap...]
  transfers between devices with their start and end apart: 1 -> 0, of which waited for: 1 -> 0; matrix products, arithmetic and copies ran while one was open for 0% -> 0% of each run, Pallas kernels for 0% -> 0%
where the time goes in v1:
time: 58.7 us; the launch traced here: 58.5 us
  Pallas kernels  56.2 us (96%)
  local copies, waits for them, and re-layouts  2.24 us (4%)
    pallas_call x1, Pallas kernels, body(): pl.pallas_call(functools.partial(kernel, n), out_shape=jax.ShapeDtypeStru...  56.2 us
    unnamed x7, local copies, waits for them, and re-layouts  2.24 us

profile of v1, /device:TPU:1, one launch (start us, length us, event | category | flops | bytes accessed | tf_op | source)
XLA Modules:
  0.0 58.5 jit_solution(17299327679065321529)
XLA Ops:
  0.0 0.0 copy-start.1
  0.0 0.9 %copy.4.phi_ref = bf16[3,128,4]{2,1,0:T(8,128)(2,1)S(1)} copy(bf16[3,128,4]{1,2,0:T(4,128)(2,1)} %param.3) | data formatting | bytes 6144 | tf_op args[0]
  0.9 0.0 copy-done.1
  0.9 0.0 copy-start
  0.9 0.2 copy.5.grad_ref
  1.1 0.5 copy-done
  1.6 56.2 %shard_map.37 = bf16[32,8,512]{2,1,0:T(8,128)(2,1)S(1)} custom-call(bf16[3,128,4]{2,1,0:T(8,128)(2,1)S(1)} %copy.4.phi_ref, bf16[8,128,32]{2,1,0:T(8,128)(2,1)S(1)} %copy.5.grad_ref, f32[1,128]{1,0:T(1,128)S(1)} %bitcast.1), custom_call_target="tpu_custom_call" | custom-call | tf_op jit(solution)/shard_map/pallas_call | solution.py:275
  57.8 0.7 %copy.7 = bf16[32,8,512]{2,1,0:T(8,128)(2,1)} copy(bf16[32,8,512]{2,1,0:T(8,128)(2,1)S(1)} %shard_map.37) | data formatting | bytes 524288
Async XLA Ops:
  0.0 0.9 %copy-start.1 = (bf16[8,128,32]{1,2,0:T(8,128)(2,1)S(1)}, bf16[8,128,32]{1,2,0:T(8,128)(2,1)}, u32[]{:S(2)}) copy-start(bf16[8,128,32]{1,2,0:T(8,128)(2,1)} %param.4) | copy-start | bytes 196612
  0.9 0.7 %copy-start = (f32[128]{0:T(128)S(1)}, f32[128]{0:T(128)}, u32[]{:S(2)}) copy-start(f32[128]{0:T(128)} %param.5) | copy-start | bytes 1540

commit v2 on v1

v2 whole, which is shorter than its diff:
```python
import functools

import jax
import jax.numpy as jnp
from jax import lax
from jax.experimental import pallas as pl
from jax.experimental.pallas import tpu as pltpu
from jax.sharding import PartitionSpec as P

MESH = pl.DeviceIdType.MESH
BF = jnp.bfloat16
F32 = jnp.float32
LANES = 128
NT = (((1,), (1,)), ((), ()))


def kernel(
    n,
    phi_hbm,
    grad_hbm,
    weight_hbm,
    out_ref,
    phi_ref,
    grad_ref,
    weight_ref,
    own_phi,
    grads,
    came_i,
    came_j,
    first,
    second,
    left,
    right,
    sent,
    landed,
    tidy,
    local,
    send,
    recv_i1,
    recv_j1,
    recv_i2,
    recv_j2,
    recv_im,
    recv_jm,
    recv_g,
    recv_o,
    ready,
):
    y = lax.axis_index("space")
    z = lax.axis_index("modej")
    mk = lax.axis_index("modek")
    x = mk // 2
    c = mk % 2
    half = n // 2
    tiles = 3 * n // 4

    def at(yy, zz, xx, cc):
        return (yy, zz, xx * 2 + cc)

    def step(v, d):
        return lax.rem(v + d, n)

    def remote(src, dst, ssem, rsem, dev):
        return pltpu.make_async_remote_copy(
            src_ref=src, dst_ref=dst, send_sem=ssem, recv_sem=rsem, device_id=dev, device_id_type=MESH
        )

    def took(ref, sem):
        pltpu.make_async_copy(ref, ref, sem).wait()

    mate = at(y, z, x, 1 - c)
    far_first = [half] + [d for k in range(half - 1, 0, -1) for d in (k, n - k)]
    opposite = lax.rem(2 * n - x - z, n)
    j_self = (x == 0) & (z == 0)
    i_self = x == y

    loads = [
        pltpu.make_async_copy(phi_hbm, phi_ref, local.at[0]),
        pltpu.make_async_copy(grad_hbm, grad_ref, local.at[1]),
        pltpu.make_async_copy(weight_hbm, weight_ref, local.at[2]),
    ]
    for load in loads:
        load.start()

    barrier = pltpu.get_barrier_semaphore()

    def hello(dev):
        pl.semaphore_signal(barrier, inc=1, device_id=dev, device_id_type=MESH)

    for d in far_first:
        @pl.when(jnp.logical_not(j_self))
        def _():
            hello(at(step(y, d), opposite, z, c))

        hello(at(step(y, d), z, y, c))
        hello(at(step(y, d), z, x, c))
        hello(at(step(y, d), z, x, 1 - c))
        hello(at(y, z, step(x, d), c))
        hello(at(y, step(z, d), x, c))

        @pl.when(j_self)
        def _():
            hello(at(step(y, d), opposite, z, c))

    @pl.when(jnp.logical_not(j_self))
    def _():
        hello(at(y, opposite, z, c))

    @pl.when(jnp.logical_not(i_self))
    def _():
        hello(at(y, z, y, c))

    hello(mate)

    for load in loads:
        load.wait()
    rows = [phi_ref[a].astype(F32) for a in range(3)]
    rows.append(jnp.zeros((4, LANES), F32))
    own_phi[...] = jnp.concatenate(rows, axis=0).astype(BF)
    weight = weight_ref[...]
    for ab in range(8):
        grads[y, ab * 32 : ab * 32 + 32, :] = (grad_ref[ab].astype(F32) * weight).astype(BF)

    pl.semaphore_wait(
        barrier, 4 * (n - 1) + 1 + 2 * n - j_self.astype(jnp.int32) - i_self.astype(jnp.int32)
    )

    for d in far_first:
        remote(own_phi, came_i.at[y], send.at[0], recv_i1, at(x, z, step(x, d), c)).start()

    @pl.when(i_self)
    def _():
        pltpu.make_async_copy(own_phi, came_i.at[y], recv_i1).start()

    @pl.when(jnp.logical_not(i_self))
    def _():
        remote(own_phi, came_i.at[y], send.at[0], recv_i1, at(x, z, x, c)).start()

    for d in far_first:
        remote(own_phi, came_j.at[y], send.at[1], recv_j1, at(step(y, d), x, opposite, c)).start()

    @pl.when(j_self)
    def _():
        pltpu.make_async_copy(own_phi, came_j.at[y], recv_j1).start()

    @pl.when(jnp.logical_not(j_self))
    def _():
        remote(own_phi, came_j.at[y], send.at[1], recv_j1, at(y, x, opposite, c)).start()

    for d in far_first:
        remote(grads.at[y], grads.at[y], send.at[6], recv_g.at[y], at(step(y, d), z, x, c)).start()
    for d in far_first:
        pl.semaphore_signal(ready, inc=1, device_id=at(y, z, step(x, d), c), device_id_type=MESH)

    row = lax.broadcasted_iota(jnp.int32, (16, LANES), 0)
    picks = [jnp.where(row // 4 == a, 1.0, 0.0).astype(BF) for a in range(4)]

    def pack(blocks, out):
        for t in range(tiles):
            moved = pltpu.roll(blocks[tiles + t // 3].astype(F32), (12 - 4 * (t % 3)) % 16, 0)
            out[t] = jnp.where(row < 12, blocks[t].astype(F32), moved).astype(BF)

    def spot(ys, a):
        return (ys, a) if ys < tiles else (3 * (ys - tiles) + a, 3)

    def build(zs, cs):
        at_row = pl.multiple_of(zs * 32 + cs * 16, 16)
        for ys in range(n):
            for a in range(3):
                t, group = spot(ys, a)
                left[pl.ds(at_row, 16), (ys * 3 + a) * LANES : (ys * 3 + a + 1) * LANES] = (
                    first[cs, zs, t] * picks[group]
                )

    def pass_i(d):
        zs = step(z, d)
        took(first.at[c, zs], recv_i2.at[zs])
        remote(first.at[c, zs], first.at[c, zs], send.at[4], recv_im.at[zs], mate).start()
        build(zs, c)

    def pass_j(xs):
        took(second.at[c, xs], recv_j2.at[xs])
        remote(second.at[c, xs], second.at[c, xs], send.at[5], recv_jm.at[xs], mate).start()

    def form(xs):
        for ys in range(n):
            g = [grads[ys, ab * 32 : ab * 32 + 32, :] for ab in range(8)]
            g.append(-(g[0] + g[4]))
            for cs in range(2):
                values = [second[cs, xs, spot(ys, b)[0]] for b in range(3)]
                for r in range(4):
                    v = []
                    for b in range(3):
                        at_r = spot(ys, b)[1] * 4 + r
                        v.append(jnp.broadcast_to(values[b][at_r : at_r + 1], (32, LANES)))
                    for a in range(3):
                        right[
                            (cs * 4 + r) * 32 : (cs * 4 + r) * 32 + 32,
                            (ys * 3 + a) * LANES : (ys * 3 + a + 1) * LANES,
                        ] = v[0] * g[3 * a] + v[1] * g[3 * a + 1] + v[2] * g[3 * a + 2]

    took(came_i, recv_i1)
    pack(came_i, first.at[c, z])
    for d in far_first:
        remote(first.at[c, z], first.at[c, z], send.at[2], recv_i2.at[z], at(y, step(z, d), x, c)).start()
    remote(first.at[c, z], first.at[c, z], send.at[4], recv_im.at[z], mate).start()
    build(z, c)
    took(came_j, recv_j1)
    pack(came_j, second.at[c, x])
    for d in far_first:
        remote(second.at[c, x], second.at[c, x], send.at[3], recv_j2.at[x], at(y, z, step(x, d), c)).start()
    remote(second.at[c, x], second.at[c, x], send.at[5], recv_jm.at[x], mate).start()

    def turn(t):
        return lax.rem(jnp.where(t % 2 == 1, (t + 1) // 2, n - t // 2), n)

    def pass_all(t, carry):
        pass_i(turn(t))
        return carry

    def build_mate(t, carry):
        zs = step(z, turn(t))
        took(first.at[1 - c, zs], recv_im.at[zs])
        build(zs, 1 - c)
        return carry

    def await_g(d, carry):
        ys = step(y, d)
        took(grads.at[ys], recv_g.at[ys])
        return carry

    def rank(dy):
        return jnp.where(dy >= half, 2 * (dy - half), 2 * (half - dy) - 1)

    own_rank = rank(lax.rem(opposite - y + n, n))

    def owner(t):
        u = jnp.where(t == 0, own_rank, jnp.where(t - 1 >= own_rank, t, t - 1))
        return lax.rem(y + jnp.where(u % 2 == 0, half + u // 2, half - (u + 1) // 2), n)

    def holder(zs):
        return lax.rem(2 * n - z - zs, n)

    lax.fori_loop(1, n, pass_all, 0)
    pass_j(holder(owner(1)))
    lax.fori_loop(1, n, await_g, 0)
    took(second.at[1 - c, x], recv_jm.at[x])
    form(x)
    lax.fori_loop(0, n, build_mate, 0)
    pl.semaphore_wait(ready, n - 1)
    owner_core = y // half
    place = lax.rem(y, half)
    low = lax.broadcasted_iota(jnp.int32, (8, 256), 0) < 4

    def chunk(t, carry):
        zs = owner(t)
        product = lax.dot_general(left[...], right[...], NT, preferred_element_type=F32)
        for xd in range(n):
            parts = []
            for cs in range(2):
                base = xd * 32 + cs * 16
                both = product[base : base + 8] + product[base + 8 : base + 16]
                parts.append(both + pltpu.roll(both, 4, 0))
            tile = jnp.where(low, parts[0], parts[1])
            tile = jnp.concatenate([tile[:, :LANES], tile[:, LANES:]], axis=0)
            sent[zs * n + xd] = tile.astype(BF)
        for d in far_first:
            xd = step(x, d)
            remote(
                sent.at[zs * n + xd], landed.at[x, place, c], send.at[7], recv_o, at(zs, z, xd, owner_core)
            ).start()
        mine = (zs == y) & (owner_core == c)

        @pl.when(mine)
        def _():
            pltpu.make_async_copy(sent.at[zs * n + x], landed.at[x, place, c], recv_o).start()

        @pl.when(jnp.logical_not(mine))
        def _():
            remote(
                sent.at[zs * n + x], landed.at[x, place, c], send.at[7], recv_o, at(zs, z, x, owner_core)
            ).start()

        @pl.when(t + 2 < n)
        def _():
            pass_j(holder(owner(t + 2)))

        @pl.when(t + 1 < n)
        def _():
            xs = holder(owner(t + 1))
            took(second.at[1 - c, xs], recv_jm.at[xs])
            form(xs)

        return carry

    lax.fori_loop(0, n, chunk, 0)

    took(landed, recv_o)

    lane = lax.broadcasted_iota(jnp.int32, (8, LANES), 1) // 32
    for p in range(half):
        for q in range(half):
            got = [landed[2 * q + s // 2, p, s % 2].astype(F32) for s in range(4)]
            for h in range(2):
                pieces = [g[h * 8 : h * 8 + 8] for g in got]
                for jl in range(4):
                    tile = pieces[jl]
                    for s in range(4):
                        if s != jl:
                            tile = jnp.where(lane == s, pltpu.roll(pieces[s], ((s - jl) * 32) % LANES, 1), tile)
                    tidy[q, pl.ds(p * 64 + h * 4 + jl, 8, stride=8), :] = tile
    for i in range(4 * n):
        for q in range(half):
            out_ref[i, :, q * LANES : (q + 1) * LANES] = tidy[q, i * 8 : i * 8 + 8, :].astype(BF)

    def left_by(flag, whole, less, sem):
        @pl.when(flag)
        def _():
            took(less, sem)

        @pl.when(jnp.logical_not(flag))
        def _():
            took(whole, sem)

    left_by(i_self, came_i, came_i.at[pl.ds(0, n - 1)], send.at[0])
    left_by(j_self, came_j, came_j.at[pl.ds(0, n - 1)], send.at[1])
    took(first.at[0, pl.ds(0, n - 1)], send.at[2])
    took(second.at[0, pl.ds(0, n - 1)], send.at[3])
    took(first.at[0], send.at[4])
    took(second.at[0], send.at[5])
    took(grads.at[pl.ds(0, n - 1)], send.at[6])
    left_by(owner_core == c, sent, sent.at[pl.ds(0, n * n - 1)], send.at[7])


def body(n, mode_shapes, mode_grads, cell_weights):
    dma = pltpu.SemaphoreType.DMA
    tiles = 3 * n // 4
    return pl.pallas_call(
        functools.partial(kernel, n),
        out_shape=jax.ShapeDtypeStruct((4 * n, 8, 64 * n), BF),
        in_specs=[pl.BlockSpec(memory_space=pl.ANY)] * 3,
        out_specs=pl.BlockSpec(memory_space=pltpu.VMEM),
        scratch_shapes=[
            pltpu.VMEM((3, 4, LANES), BF),
            pltpu.VMEM((8, 32, LANES), BF),
            pltpu.VMEM((1, LANES), F32),
            pltpu.VMEM((16, LANES), BF),
            pltpu.VMEM((n, 256, LANES), BF),
            pltpu.VMEM((n, 16, LANES), BF),
            pltpu.VMEM((n, 16, LANES), BF),
            pltpu.VMEM((2, n, tiles, 16, LANES), BF),
            pltpu.VMEM((2, n, tiles, 16, LANES), BF),
            pltpu.VMEM((32 * n, 3 * n * LANES), BF),
            pltpu.VMEM((256, 3 * n * LANES), BF),
            pltpu.VMEM((n * n, 16, LANES), BF),
            pltpu.VMEM((n, n // 2, 2, 16, LANES), BF),
            pltpu.VMEM((n // 2, 32 * n, LANES), F32),
            dma((3,)),
            dma((8,)),
            dma(()),
            dma(()),
            dma((n,)),
            dma((n,)),
            dma((n,)),
            dma((n,)),
            dma((n,)),
            dma(()),
            pltpu.SemaphoreType.REGULAR,
        ],
        compiler_params=pltpu.CompilerParams(
            collective_id=0, has_side_effects=True, vmem_limit_bytes=56 * 2**20
        ),
    )(
        jnp.transpose(mode_shapes, (0, 2, 1)),
        jnp.transpose(mode_grads, (0, 2, 1)),
        cell_weights.reshape(1, -1),
    )


def solution(mesh):
    n = mesh.shape["space"]
    in_specs = (P(None, "space", ("modej", "modek")), P(None, "space", "modek"), P("space"))
    out_specs = P("modek", ("space", "modej"), None)
    return jax.shard_map(
        functools.partial(body, n), mesh=mesh, in_specs=in_specs, out_specs=out_specs, check_vma=False
    )
```

time: 58.7 us -> 54.5 us (0.928)
  Pallas kernels: 56.2 us -> 52.6 us
    pallas_call x1, Pallas kernels: 56.2 us -> 52.6 us  [body(): pl.pallas_call(functools.partial(kernel, n), out_shape=jax.ShapeDtypeStru...]
    unnamed x7 -> x1, local copies, waits for them, and re-layouts: 2.24 us -> 1.67 us
where the time goes in v2:
time: 54.5 us; the launch traced here: 54.3 us
  Pallas kernels  52.6 us (97%)
  local copies, waits for them, and re-layouts  1.67 us (3%)
    pallas_call x1, Pallas kernels, body(): pl.pallas_call(functools.partial(kernel, n), out_shape=jax.ShapeDtypeStru...  52.6 us
    unnamed x1, local copies, waits for them, and re-layouts  1.67 us

profile of v2, /device:TPU:1, one launch (start us, length us, event | category | flops | bytes accessed | tf_op | source)
XLA Modules:
  0.0 54.3 jit_solution(18005496774646249601)
XLA Ops:
  0.0 52.6 %shard_map.37 = bf16[32,8,512]{2,1,0:T(8,128)(2,1)} custom-call(bf16[3,4,128]{2,1,0:T(4,128)(2,1)} %bitcast.4, bf16[8,32,128]{2,1,0:T(8,128)(2,1)} %bitcast.3, f32[1,128]{1,0:T(1,128)} %bitcast.5), custom_call_target="tpu_custom_call" | custom-call | tf_op jit(solution)/shard_map/pallas_call | solution.py:338
  52.6 1.7 %copy.5 = bf16[32,8,512]{2,1,0:T(8,128)(2,1)} copy(bf16[32,8,512]{2,1,0:T(8,128)(2,1)} %shard_map.37) | data formatting | bytes 524288

commit v3 on v2

v3 whole, which is shorter than its diff:
```python
import functools

import jax
import jax.numpy as jnp
from jax import lax
from jax.experimental import pallas as pl
from jax.experimental.pallas import tpu as pltpu
from jax.sharding import PartitionSpec as P

MESH = pl.DeviceIdType.MESH
BF = jnp.bfloat16
F32 = jnp.float32
LANES = 128
NT = (((1,), (1,)), ((), ()))


def kernel(
    n,
    phi_hbm,
    grad_hbm,
    weight_hbm,
    landed,
    phi_ref,
    grad_ref,
    weight_ref,
    own_phi,
    grads,
    came_i,
    came_j,
    first,
    second,
    left,
    right,
    sent,
    local,
    send,
    recv_i1,
    recv_j1,
    recv_i2,
    recv_j2,
    recv_im,
    recv_jm,
    recv_g,
    recv_o,
    ready,
):
    y = lax.axis_index("space")
    z = lax.axis_index("modej")
    mk = lax.axis_index("modek")
    x = mk // 2
    c = mk % 2
    half = n // 2
    per = (3 * half + 3) // 4

    def at(yy, zz, xx, cc):
        return (yy, zz, xx * 2 + cc)

    def step(v, d):
        return lax.rem(v + d, n)

    def remote(src, dst, ssem, rsem, dev):
        return pltpu.make_async_remote_copy(
            src_ref=src, dst_ref=dst, send_sem=ssem, recv_sem=rsem, device_id=dev, device_id_type=MESH
        )

    def took(ref, sem):
        pltpu.make_async_copy(ref, ref, sem).wait()

    mate = at(y, z, x, 1 - c)
    far_first = [half] + [d for k in range(half - 1, 0, -1) for d in (k, n - k)]
    near_first = far_first[::-1]
    members = [[(g * half - n // 4 + k) % n for k in range(half)] for g in range(2)]
    group = lax.rem(y + n // 4, n) // half
    opposite = lax.rem(2 * n - x - z, n)
    j_self = (x == 0) & (z == 0)
    i_self = x == y

    loads = [
        pltpu.make_async_copy(phi_hbm, phi_ref, local.at[0]),
        pltpu.make_async_copy(grad_hbm, grad_ref, local.at[1]),
        pltpu.make_async_copy(weight_hbm, weight_ref, local.at[2]),
    ]
    for load in loads:
        load.start()

    barrier = pltpu.get_barrier_semaphore()

    def hello(dev):
        pl.semaphore_signal(barrier, inc=1, device_id=dev, device_id_type=MESH)

    for d in far_first:
        hello(at(step(y, d), opposite, z, c))
    for d in far_first:
        hello(at(step(y, d), z, y, c))

    @pl.when(jnp.logical_not(j_self))
    def _():
        hello(at(y, opposite, z, c))

    @pl.when(jnp.logical_not(i_self))
    def _():
        hello(at(y, z, y, c))

    for d in far_first:
        hello(at(step(y, d), z, x, c))
        hello(at(y, z, step(x, d), c))
        hello(at(y, step(z, d), x, c))
    for d in far_first:
        hello(at(step(y, d), z, x, 1 - c))
    hello(mate)

    loads[0].wait()
    rows = [phi_ref[a].astype(F32) for a in range(3)]
    rows.append(jnp.zeros((4, LANES), F32))
    own_phi[...] = jnp.concatenate(rows, axis=0).astype(BF)

    pl.semaphore_wait(
        barrier, 4 * (n - 1) + 1 + 2 * n - j_self.astype(jnp.int32) - i_self.astype(jnp.int32)
    )

    for d in far_first:
        remote(own_phi, came_i.at[y], send.at[0], recv_i1.at[group], at(x, z, step(x, d), c)).start()

    @pl.when(i_self)
    def _():
        pltpu.make_async_copy(own_phi, came_i.at[y], recv_i1.at[group]).start()

    @pl.when(jnp.logical_not(i_self))
    def _():
        remote(own_phi, came_i.at[y], send.at[0], recv_i1.at[group], at(x, z, x, c)).start()

    for d in far_first:
        remote(own_phi, came_j.at[y], send.at[1], recv_j1.at[group], at(step(y, d), x, opposite, c)).start()

    @pl.when(j_self)
    def _():
        pltpu.make_async_copy(own_phi, came_j.at[y], recv_j1.at[group]).start()

    @pl.when(jnp.logical_not(j_self))
    def _():
        remote(own_phi, came_j.at[y], send.at[1], recv_j1.at[group], at(y, x, opposite, c)).start()

    loads[1].wait()
    loads[2].wait()
    weight = weight_ref[...]
    for ab in range(8):
        grads[y, ab * 32 : ab * 32 + 32, :] = (grad_ref[ab].astype(F32) * weight).astype(BF)

    for d in far_first:
        remote(grads.at[y], grads.at[y], send.at[6], recv_g.at[y], at(step(y, d), z, x, c)).start()
    for d in far_first:
        pl.semaphore_signal(ready, inc=1, device_id=at(y, z, step(x, d), c), device_id_type=MESH)

    row = lax.broadcasted_iota(jnp.int32, (16, LANES), 0)
    picks = [jnp.where(row // 4 == a, 1.0, 0.0).astype(BF) for a in range(4)]

    spots = {}
    for g in range(2):
        for k, ys in enumerate(members[g]):
            for a in range(3):
                if k < per:
                    spots[ys, a] = (per * g + k, a)
                else:
                    spots[ys, a] = (per * g + 3 * (k - per) + a, 3)

    def pack(blocks, out, g):
        for k in range(per):
            block = blocks[members[g][k]]
            if per < half:
                moved = pltpu.roll(blocks[members[g][per + k // 3]].astype(F32), (12 - 4 * (k % 3)) % 16, 0)
                block = jnp.where(row < 12, block.astype(F32), moved).astype(BF)
            out[per * g + k] = block

    def build(zs, cs):
        at_row = pl.multiple_of(zs * 32 + cs * 16, 16)
        for ys in range(n):
            for a in range(3):
                t, quad = spots[ys, a]
                left[pl.ds(at_row, 16), (ys * 3 + a) * LANES : (ys * 3 + a + 1) * LANES] = (
                    first[cs, zs, t] * picks[quad]
                )

    def part(ref, core, at_v, g):
        return ref.at[core, at_v, pl.ds(per * g, per)]

    def pass_i(zs):
        for g in range(2):
            block = part(first, c, zs, g)
            took(block, recv_i2.at[zs, g])
            remote(block, block, send.at[4], recv_im.at[zs, g], mate).start()
        build(zs, c)

    def pass_j(xs):
        for g in range(2):
            block = part(second, c, xs, g)
            took(block, recv_j2.at[xs, g])
            remote(block, block, send.at[5], recv_jm.at[xs, g], mate).start()

    def form(xs, await_block=None):
        for ys in range(n):
            if await_block is not None:
                await_block(ys)
            g = [grads[ys, ab * 32 : ab * 32 + 32, :] for ab in range(8)]
            g.append(-(g[0] + g[4]))
            for cs in range(2):
                values = [second[cs, xs, spots[ys, b][0]] for b in range(3)]
                for r in range(4):
                    v = []
                    for b in range(3):
                        at_r = spots[ys, b][1] * 4 + r
                        v.append(jnp.broadcast_to(values[b][at_r : at_r + 1], (32, LANES)))
                    for a in range(3):
                        right[
                            (cs * 4 + r) * 32 : (cs * 4 + r) * 32 + 32,
                            (ys * 3 + a) * LANES : (ys * 3 + a + 1) * LANES,
                        ] = v[0] * g[3 * a] + v[1] * g[3 * a + 1] + v[2] * g[3 * a + 2]

    for g in range(2):
        took(came_i.at[pl.ds(0, half)], recv_i1.at[g])
        pack(came_i, first.at[c, z], g)
        block = part(first, c, z, g)
        for d in near_first:
            remote(block, block, send.at[2], recv_i2.at[z, g], at(y, step(z, d), x, c)).start()
        remote(block, block, send.at[4], recv_im.at[z, g], mate).start()
        took(came_j.at[pl.ds(0, half)], recv_j1.at[g])
        pack(came_j, second.at[c, x], g)
        block = part(second, c, x, g)
        for d in near_first:
            remote(block, block, send.at[3], recv_j2.at[x, g], at(y, z, step(x, d), c)).start()
        remote(block, block, send.at[5], recv_jm.at[x, g], mate).start()
    build(z, c)

    def turn(t):
        return lax.rem(jnp.where(t % 2 == 1, (t + 1) // 2, n - t // 2), n)

    def build_mate(zs, carry):
        for g in range(2):
            took(part(first, 1 - c, zs, g), recv_im.at[zs, g])
        build(zs, 1 - c)
        return carry

    def await_g(ys):
        @pl.when(ys != y)
        def _():
            took(grads.at[ys], recv_g.at[ys])

    def rank(dy):
        return jnp.where(dy >= half, 2 * (dy - half), 2 * (half - dy) - 1)

    own_rank = rank(lax.rem(opposite - y + n, n))

    def owner(t):
        u = jnp.where(t == 0, own_rank, jnp.where(t - 1 >= own_rank, t, t - 1))
        return lax.rem(y + jnp.where(u % 2 == 0, half + u // 2, half - (u + 1) // 2), n)

    def holder(zs):
        return lax.rem(2 * n - z - zs, n)

    def pass_all(t, carry):
        pass_i(step(z, turn(t)))
        return carry

    lax.fori_loop(1, n, pass_all, 0)
    pass_j(holder(owner(1)))
    for g in range(2):
        took(part(second, 1 - c, x, g), recv_jm.at[x, g])
    form(x, await_g)
    lax.fori_loop(0, n, build_mate, 0)
    pl.semaphore_wait(ready, n - 1)
    owner_core = y // half
    place = lax.rem(y, half)
    low = lax.broadcasted_iota(jnp.int32, (8, 256), 0) < 4

    def chunk(t, carry):
        zs = owner(t)
        product = lax.dot_general(left[...], right[...], NT, preferred_element_type=F32)
        for xd in range(n):
            parts = []
            for cs in range(2):
                base = xd * 32 + cs * 16
                both = product[base : base + 8] + product[base + 8 : base + 16]
                parts.append(both + pltpu.roll(both, 4, 0))
            tile = jnp.where(low, parts[0], parts[1])
            tile = jnp.concatenate([tile[:, :LANES], tile[:, LANES:]], axis=0)
            sent[zs * n + xd] = tile.astype(BF)
        for d in far_first:
            xd = step(x, d)
            remote(
                sent.at[zs * n + xd], landed.at[x, place, c], send.at[7], recv_o, at(zs, z, xd, owner_core)
            ).start()
        mine = (zs == y) & (owner_core == c)

        @pl.when(mine)
        def _():
            pltpu.make_async_copy(sent.at[zs * n + x], landed.at[x, place, c], recv_o).start()

        @pl.when(jnp.logical_not(mine))
        def _():
            remote(
                sent.at[zs * n + x], landed.at[x, place, c], send.at[7], recv_o, at(zs, z, x, owner_core)
            ).start()

        @pl.when(t + 2 < n)
        def _():
            pass_j(holder(owner(t + 2)))

        @pl.when(t + 1 < n)
        def _():
            xs = holder(owner(t + 1))
            for g in range(2):
                took(part(second, 1 - c, xs, g), recv_jm.at[xs, g])
            form(xs)

        return carry

    lax.fori_loop(0, n, chunk, 0)

    took(landed, recv_o)

    def left_by(flag, whole, less, sem):
        @pl.when(flag)
        def _():
            took(less, sem)

        @pl.when(jnp.logical_not(flag))
        def _():
            took(whole, sem)

    left_by(i_self, came_i, came_i.at[pl.ds(0, n - 1)], send.at[0])
    left_by(j_self, came_j, came_j.at[pl.ds(0, n - 1)], send.at[1])
    took(first.at[0, pl.ds(0, n - 1)], send.at[2])
    took(second.at[0, pl.ds(0, n - 1)], send.at[3])
    took(first.at[0], send.at[4])
    took(second.at[0], send.at[5])
    took(grads.at[pl.ds(0, n - 1)], send.at[6])
    left_by(owner_core == c, sent, sent.at[pl.ds(0, n * n - 1)], send.at[7])


def arrange(n, landed, out_ref, tidy):
    half = n // 2
    lane = lax.broadcasted_iota(jnp.int32, (8, LANES), 1) // 32
    for p in range(half):
        for q in range(half):
            got = [landed[2 * q + s // 2, p, s % 2].astype(F32) for s in range(4)]
            for h in range(2):
                pieces = [g[h * 8 : h * 8 + 8] for g in got]
                for jl in range(4):
                    tile = pieces[jl]
                    for s in range(4):
                        if s != jl:
                            tile = jnp.where(lane == s, pltpu.roll(pieces[s], ((s - jl) * 32) % LANES, 1), tile)
                    tidy[q, pl.ds(p * 64 + h * 4 + jl, 8, stride=8), :] = tile
    for i in range(4 * n):
        for q in range(half):
            out_ref[i, :, q * LANES : (q + 1) * LANES] = tidy[q, i * 8 : i * 8 + 8, :].astype(BF)


def body(n, mode_shapes, mode_grads, cell_weights):
    dma = pltpu.SemaphoreType.DMA
    tiles = 2 * ((3 * (n // 2) + 3) // 4)
    parts = pl.pallas_call(
        functools.partial(kernel, n),
        out_shape=jax.ShapeDtypeStruct((n, n // 2, 2, 16, LANES), BF),
        in_specs=[pl.BlockSpec(memory_space=pl.ANY)] * 3,
        out_specs=pl.BlockSpec(memory_space=pl.ANY),
        scratch_shapes=[
            pltpu.VMEM((3, 4, LANES), BF),
            pltpu.VMEM((8, 32, LANES), BF),
            pltpu.VMEM((1, LANES), F32),
            pltpu.VMEM((16, LANES), BF),
            pltpu.VMEM((n, 256, LANES), BF),
            pltpu.VMEM((n, 16, LANES), BF),
            pltpu.VMEM((n, 16, LANES), BF),
            pltpu.VMEM((2, n, tiles, 16, LANES), BF),
            pltpu.VMEM((2, n, tiles, 16, LANES), BF),
            pltpu.VMEM((32 * n, 3 * n * LANES), BF),
            pltpu.VMEM((256, 3 * n * LANES), BF),
            pltpu.VMEM((n * n, 16, LANES), BF),
            dma((3,)),
            dma((8,)),
            dma((2,)),
            dma((2,)),
            dma((n, 2)),
            dma((n, 2)),
            dma((n, 2)),
            dma((n, 2)),
            dma((n,)),
            dma(()),
            pltpu.SemaphoreType.REGULAR,
        ],
        compiler_params=pltpu.CompilerParams(
            collective_id=0, has_side_effects=True, vmem_limit_bytes=56 * 2**20
        ),
    )(
        jnp.transpose(mode_shapes, (0, 2, 1)),
        jnp.transpose(mode_grads, (0, 2, 1)),
        cell_weights.reshape(1, -1),
    )
    return pl.pallas_call(
        functools.partial(arrange, n),
        out_shape=jax.ShapeDtypeStruct((4 * n, 8, 64 * n), BF),
        in_specs=[pl.BlockSpec(memory_space=pltpu.VMEM)],
        out_specs=pl.BlockSpec(memory_space=pltpu.VMEM),
        scratch_shapes=[pltpu.VMEM((n // 2, 32 * n, LANES), F32)],
    )(parts)


def solution(mesh):
    n = mesh.shape["space"]
    in_specs = (P(None, "space", ("modej", "modek")), P(None, "space", "modek"), P("space"))
    out_specs = P("modek", ("space", "modej"), None)
    return jax.shard_map(
        functools.partial(body, n), mesh=mesh, in_specs=in_specs, out_specs=out_specs, check_vma=False
    )
```

time: 54.5 us -> 54.1 us (level)
  local copies, waits for them, and re-layouts: 1.67 us -> 0 us
  Pallas kernels: 52.6 us -> 53.9 us
    pallas_call x0 -> x1, Pallas kernels: none -> 1.95 us  [body(): pl.pallas_call(functools.partial(arrange, n), out_shape=jax.ShapeDtypeStr...]
    unnamed x1 -> x0, local copies, waits for them, and re-layouts: 1.67 us -> none
    pallas_call x1, Pallas kernels: 52.6 us -> 51.9 us  [body(): pl.pallas_call(functools.partial(kernel, n), out_shape=jax.ShapeDtypeStru...]
where the time goes in v3:
time: 54.1 us; the launch traced here: 53.9 us
  Pallas kernels  53.9 us (100%)
    pallas_call x1, Pallas kernels, body(): pl.pallas_call(functools.partial(kernel, n), out_shape=jax.ShapeDtypeStru...  51.9 us
    pallas_call x1, Pallas kernels, body(): pl.pallas_call(functools.partial(arrange, n), out_shape=jax.ShapeDtypeStr...  1.95 us

profile of v3, /device:TPU:1, one launch (start us, length us, event | category | flops | bytes accessed | tf_op | source)
XLA Modules:
  0.0 53.9 jit_solution(7402914181446728465)
XLA Ops:
  0.0 51.9 %shard_map.37.landed = bf16[8,4,2,16,128]{4,3,2,1,0:T(8,128)(2,1)} custom-call(bf16[3,4,128]{2,1,0:T(4,128)(2,1)} %bitcast.4, bf16[8,32,128]{2,1,0:T(8,128)(2,1)} %bitcast.3, f32[1,128]{1,0:T(1,128)} %bitcast.5), custom_call_target="tpu_custom_call" | custom-call | tf_op jit(solution)/shard_map/pallas_call | solution.py:361
  51.9 2.0 %shard_map.38 = bf16[32,8,512]{2,1,0:T(8,128)(2,1)} custom-call(bf16[8,4,2,16,128]{4,3,2,1,0:T(8,128)(2,1)} %shard_map.37.landed), custom_call_target="tpu_custom_call" | custom-call | tf_op jit(solution)/shard_map/pallas_call | solution.py:399
